TPU v7x, 32 devices: a whole 2x2x4 slice. The times are simulated.
32 devices in a mesh: dp: 8 (over z, y), mp: 4 (over x, core).
Axes of the slice: x: 2, y: 2, z: 4, core: 2. Of those that a mesh axis runs over, the one named last changes fastest.
Arguments:
- tokens: bfloat16 [4096, 1152], P(('dp', 'mp')), may hold values from -6 to 6
- segment_ids: int32 [4096], P('dp'), may hold values from 0 to 2, as said below
- positions: int32 [4096], P('dp'), may hold values from 0 to 5118, as said below
- q_weight: bfloat16 [1152, 1024], P('dp', 'mp'), may hold values from -0.1875 to 0.1875
- kv_weight: bfloat16 [1152, 512], P('dp'), may hold values from -0.1875 to 0.1875
- o_weight: bfloat16 [1024, 1152], P('mp', 'dp'), may hold values from -0.1875 to 0.1875
- gate_up_weight: bfloat16 [2, 1152, 6912], P(None, 'dp', 'mp'), may hold values from -0.1875 to 0.1875
- down_weight: bfloat16 [6912, 1152], P('mp', 'dp'), may hold values from -0.078125 to 0.078125
- attn_pre_gain: bfloat16 [1152], P('dp'), may hold values from 0.25 to 1.75
- attn_post_gain: bfloat16 [1152], P('dp'), may hold values from 0.25 to 1.75
- ff_pre_gain: bfloat16 [1152], P('dp'), may hold values from 0.25 to 1.75
- ff_post_gain: bfloat16 [1152], P('dp'), may hold values from 0.25 to 1.75
- query_gain: bfloat16 [256], P('dp'), may hold values from 0.25 to 1.75
- key_gain: bfloat16 [256], P('dp'), may hold values from 0.25 to 1.75
- out_grad: bfloat16 [4096, 1152], P(('dp', 'mp')), may hold values from -6 to 6
Outputs:
- out: bfloat16 [4096, 1152], P(('dp', 'mp'))
- tokens_grad: float32 [4096, 1152], P(('dp', 'mp'))
- q_weight_grad: float32 [1152, 1024], P('dp', 'mp')
- kv_weight_grad: float32 [1152, 512], P('dp')
- o_weight_grad: float32 [1024, 1152], P('mp', 'dp')
- gate_up_weight_grad: float32 [2, 1152, 6912], P(None, 'dp', 'mp')
- down_weight_grad: float32 [6912, 1152], P('mp', 'dp')
- attn_pre_gain_grad: float32 [1152], P('dp')
- attn_post_gain_grad: float32 [1152], P('dp')
- ff_pre_gain_grad: float32 [1152], P('dp')
- ff_post_gain_grad: float32 [1152], P('dp')
- query_gain_grad: float32 [256], P('dp')
- key_gain_grad: float32 [256], P('dp')
Inputs may be any that keep to these rules, and one draw needn't show every extreme that they name: `segment_ids`: segment ids never fall; document 0 and document 2 each hold 1 to 256 tokens, document 1 the rest. Within a document, positions rise by one from token to token; document 0 starts at position 0, document 2 at 0 to 1023, and the last token of document 1 has position 5118.
All inputs are finite; a program needn't handle non-finite values.
Results may differ from a plain program's by a relative error of at most 0.028.
Values may be sent and summed in bfloat16 or wider, within the bound.
A program may use at most 128 MiB of HBM per device.

v0:
```python
from functools import partial
import jax
import jax.numpy as jnp
from jax import lax
from jax.sharding import PartitionSpec as P

WINDOW = 512
EPS = 1e-06
NEG = -1e30


def from_behind(value, axis, steps):
    count = lax.axis_size(axis)
    leading, last = (max(0, -steps), min(count, count - steps))
    return lax.ppermute(value, axis, [(source, source + steps) for source in range(leading, last)])


def shifted(value, axis, shift):
    count = lax.axis_size(axis)
    return lax.ppermute(value, axis, [(i, (i + shift) % count) for i in range(count)])


def gather_relative(value):
    count = lax.axis_size("mp")
    return [value] + [shifted(value, "mp", -step) for step in range(1, count)]


def gather_ordered(value):
    count = lax.axis_size("mp")
    rows = value.shape[0]
    me = lax.axis_index("mp")
    whole = jnp.zeros((count * rows,) + value.shape[1:], value.dtype)
    for step, block in enumerate(gather_relative(value)):
        owner = lax.rem(me + step, count)
        whole = lax.dynamic_update_slice_in_dim(whole, block, owner * rows, axis=0)
    return whole


def scatter_relative(blocks):
    total = blocks[0].astype(jnp.float32)
    for step in range(1, len(blocks)):
        total = total + shifted(blocks[step], "mp", step).astype(jnp.float32)
    return total


def scatter_ordered(value):
    count = lax.axis_size("mp")
    rows = value.shape[0] // count
    me = lax.axis_index("mp")
    return scatter_relative(
        [
            lax.dynamic_slice_in_dim(value, lax.rem(me + step, count) * rows, rows, axis=0)
            for step in range(count)
        ]
    )


def split_rows(value):
    rows = value.shape[0] // lax.axis_size("mp")
    return [value[i * rows : (i + 1) * rows] for i in range(lax.axis_size("mp"))]


def sum_over_mp(value):
    total = value.astype(jnp.float32)
    for step in range(1, lax.axis_size("mp")):
        total = total + shifted(value, "mp", step).astype(jnp.float32)
    return total


def normalize(value, gain):
    return value * lax.rsqrt(jnp.mean(value * value, axis=-1, keepdims=True) + EPS) * gain


def rotary_tables(positions, width):
    half_width = width // 2
    frequency = jnp.power(10000.0, -jnp.arange(half_width, dtype=jnp.float32) * (2.0 / width))
    angles = positions.astype(jnp.float32)[:, None] * frequency[None, :]
    return (jnp.cos(angles), jnp.sin(angles))


def rotate(value, cosine, sine):
    half_width = value.shape[-1] // 2
    first_half = value[..., :half_width]
    second_half = value[..., half_width:]
    return jnp.concatenate(
        [first_half * cosine - second_half * sine, second_half * cosine + first_half * sine],
        axis=-1,
    )


def prepare_head(pre_value, gain, cosine, sine):
    return rotate(normalize(pre_value, gain), cosine, sine)


def gated_units(gate, up_part):
    return jax.nn.gelu(gate, approximate=True) * up_part


def norm_back(value, gain, grad):
    unused, pull = jax.vjp(normalize, value, gain)
    return pull(grad)


def local(
    tokens,
    segment_ids,
    positions,
    q_weight,
    kv_weight,
    o_weight,
    gate_up_weight,
    down_weight,
    attn_pre_gain,
    attn_post_gain,
    ff_pre_gain,
    ff_post_gain,
    query_gain,
    key_gain,
    out_grad,
):
    rows = q_weight.shape[0]
    head_size = q_weight.shape[1]
    width = rows * lax.axis_size("dp")
    gain_rows = query_gain.shape[0]
    small_gains = [jnp.pad(item, (0, rows - gain_rows)) for item in (query_gain, key_gain)]
    gain_columns = jnp.stack(
        [attn_pre_gain, attn_post_gain, ff_pre_gain, ff_post_gain] + small_gains, axis=1
    )
    gain_columns = jnp.pad(gain_columns, ((0, 0), (0, 128 - gain_columns.shape[1])))
    packed = jnp.concatenate([q_weight, kv_weight, jnp.transpose(o_weight), gain_columns], axis=1)
    packed_full = lax.all_gather(packed, "dp", axis=0, tiled=True)
    gate_up_full = lax.all_gather(gate_up_weight, "dp", axis=1, tiled=True)
    down_full = lax.all_gather(down_weight, "dp", axis=1, tiled=True)
    joint_weight = packed_full[:, : 3 * head_size]
    output_turned = packed_full[:, 3 * head_size : 4 * head_size]
    gain_block = jnp.transpose(packed_full[:, 4 * head_size :]).astype(jnp.float32)
    gains = [gain_block[i] for i in range(4)] + [
        gain_block[i].reshape(-1, rows)[:, :gain_rows].reshape(-1) for i in (4, 5)
    ]
    length = segment_ids.shape[0]
    reach = -(-WINDOW // length)
    block_size = min(512, length)
    score_scale = head_size ** (-0.5)
    span = block_size + WINDOW
    cosine, sine = rotary_tables(positions, head_size)
    distance = (
        jnp.arange(block_size, dtype=jnp.int32)[:, None]
        + WINDOW
        - jnp.arange(span, dtype=jnp.int32)[None, :]
    )
    inside = (distance >= 0) & (distance < WINDOW)
    residual = tokens.astype(jnp.float32)
    attn_local = normalize(residual, gains[0]).astype(jnp.bfloat16)
    attn_in = gather_ordered(attn_local)
    projected = jnp.dot(attn_in, joint_weight, preferred_element_type=jnp.float32)
    query_pre = projected[:, :head_size]
    key_pre = projected[:, head_size : 2 * head_size]
    value_pre = projected[:, 2 * head_size :]
    queries = prepare_head(query_pre, gains[4], cosine, sine).astype(jnp.bfloat16)
    keys = prepare_head(key_pre, gains[5], cosine, sine).astype(jnp.bfloat16)
    values = value_pre.astype(jnp.bfloat16)
    marks = (segment_ids + 1).astype(jnp.bfloat16)
    key_parts, value_parts, mark_parts = ([], [], [])
    step = 1
    moved = from_behind((keys, values, marks), "dp", step)
    key_parts.append(moved[0])
    value_parts.append(moved[1])
    mark_parts.append(moved[2])
    all_keys = jnp.concatenate(key_parts + [keys], axis=0)
    all_values = jnp.concatenate(value_parts + [values], axis=0)
    all_marks = jnp.concatenate(mark_parts + [marks], axis=0)

    def block_parts(start):
        first_key = start + reach * length - WINDOW
        visible = inside & (marks[:, None] == all_marks[None, :])
        product = (
            jnp.einsum("qd,kd->qk", queries, all_keys, preferred_element_type=jnp.float32)
            * score_scale
        )
        return (first_key, queries, all_keys, all_values, jnp.where(visible, product, NEG))

    mixed_parts, total_parts = ([], [])
    start = 0
    first_key, query_block, key_block, value_block, scores = block_parts(start)
    highest = jnp.max(scores, axis=-1, keepdims=True)
    expo = jnp.exp(scores - highest)
    denominator = jnp.sum(expo, axis=-1, keepdims=True)
    probs = (expo / denominator).astype(jnp.bfloat16)
    mixed_parts.append(jnp.dot(probs, value_block, preferred_element_type=jnp.float32))
    total_parts.append(highest + jnp.log(denominator))
    attended = mixed_parts[0].astype(jnp.bfloat16)
    log_totals = total_parts[0]
    attn_out = scatter_ordered(
        jnp.einsum("le,de->ld", attended, output_turned, preferred_element_type=jnp.float32).astype(
            jnp.bfloat16
        )
    )
    middle = residual + normalize(attn_out, gains[1])
    ff_local = normalize(middle, gains[2]).astype(jnp.bfloat16)
    ff_in = jnp.concatenate(gather_relative(ff_local), axis=0)
    gate = jnp.dot(ff_in, gate_up_full[0], preferred_element_type=jnp.float32)
    up_part = jnp.dot(ff_in, gate_up_full[1], preferred_element_type=jnp.float32)
    hidden = gated_units(gate, up_part).astype(jnp.bfloat16)
    ff_out = scatter_relative(
        split_rows(
            jnp.dot(hidden, down_full, preferred_element_type=jnp.float32).astype(jnp.bfloat16)
        )
    )
    result = (middle + normalize(ff_out, gains[3])).astype(jnp.bfloat16)
    top_grad = out_grad.astype(jnp.float32)
    ff_out_grad, ff_post_grad = norm_back(ff_out, gains[3], top_grad)
    ff_grad_all = jnp.concatenate(gather_relative(ff_out_grad.astype(jnp.bfloat16)), axis=0)
    hidden_grad = jnp.einsum(
        "ld,fd->lf", ff_grad_all, down_full, preferred_element_type=jnp.float32
    )
    down_grad_turned = jnp.einsum(
        "ld,lf->df", ff_grad_all, hidden, preferred_element_type=jnp.float32
    )
    unused, unit_pull = jax.vjp(gated_units, gate, up_part)
    gate_grad, up_grad = unit_pull(hidden_grad)
    gate_low = gate_grad.astype(jnp.bfloat16)
    up_low = up_grad.astype(jnp.bfloat16)
    gate_turned = jnp.einsum("ld,lf->df", ff_in, gate_low, preferred_element_type=jnp.float32)
    up_turned = jnp.einsum("ld,lf->df", ff_in, up_low, preferred_element_type=jnp.float32)
    ff_in_partial = (
        jnp.einsum("lf,df->ld", gate_low, gate_up_full[0], preferred_element_type=jnp.float32)
        + jnp.einsum("lf,df->ld", up_low, gate_up_full[1], preferred_element_type=jnp.float32)
    ).astype(jnp.bfloat16)
    ff_in_partial, down_low, gate_turned_low, up_turned_low = lax.optimization_barrier(
        (
            ff_in_partial,
            down_grad_turned.astype(jnp.bfloat16),
            gate_turned.astype(jnp.bfloat16),
            up_turned.astype(jnp.bfloat16),
        )
    )
    feed_forward_owned = tuple(
        (
            lax.psum_scatter(item, "dp", scatter_dimension=0, tiled=True)
            for item in (down_low, gate_turned_low, up_turned_low)
        )
    )
    ff_in_grad = scatter_relative(split_rows(ff_in_partial))
    middle_part, ff_pre_grad = norm_back(middle, gains[2], ff_in_grad)
    middle_grad = top_grad + middle_part
    attn_out_grad, attn_post_grad = norm_back(attn_out, gains[1], middle_grad)
    attn_grad_all = gather_ordered(attn_out_grad.astype(jnp.bfloat16))
    attended_grad = jnp.einsum(
        "ld,de->le", attn_grad_all, output_turned, preferred_element_type=jnp.float32
    ).astype(jnp.bfloat16)
    output_grad_turned = jnp.einsum(
        "ld,le->de", attn_grad_all, attended, preferred_element_type=jnp.float32
    )
    key_grad_all = jnp.zeros(((reach + 1) * length, head_size), jnp.float32)
    value_grad_all = jnp.zeros(((reach + 1) * length, head_size), jnp.float32)
    start = 0
    first_key, query_block, key_block, value_block, scores = block_parts(start)
    probs = jnp.exp(scores - log_totals)
    probs_low = probs.astype(jnp.bfloat16)
    value_grad_all = value_grad_all.at[first_key : first_key + span].add(
        jnp.einsum("qk,qd->kd", probs_low, attended_grad, preferred_element_type=jnp.float32)
    )
    prob_grad = jnp.einsum(
        "qd,kd->qk", attended_grad, value_block, preferred_element_type=jnp.float32
    )
    inner = jnp.sum(probs * prob_grad, axis=-1, keepdims=True)
    score_grad = (probs * (prob_grad - inner)).astype(jnp.bfloat16)
    query_parts = jnp.dot(score_grad, key_block, preferred_element_type=jnp.float32) * score_scale
    key_grad_all = key_grad_all.at[first_key : first_key + span].add(
        jnp.einsum("qk,qd->kd", score_grad, query_block, preferred_element_type=jnp.float32)
        * score_scale
    )
    own_keys = key_grad_all[reach * length :]
    own_values = value_grad_all[reach * length :]
    step = 1
    slot = reach - step
    returned = (
        from_behind(
            key_grad_all[slot * length : (slot + 1) * length].astype(jnp.bfloat16), "dp", -step
        ).astype(jnp.float32),
        from_behind(
            value_grad_all[slot * length : (slot + 1) * length].astype(jnp.bfloat16), "dp", -step
        ).astype(jnp.float32),
    )
    own_keys = own_keys + returned[0]
    own_values = own_values + returned[1]
    unused, query_pull = jax.vjp(
        partial(prepare_head, cosine=cosine, sine=sine), query_pre, gains[4]
    )
    query_pre_grad, query_gain_grad = query_pull(query_parts)
    unused, key_pull = jax.vjp(partial(prepare_head, cosine=cosine, sine=sine), key_pre, gains[5])
    key_pre_grad, key_gain_grad = key_pull(own_keys)
    joint_grad_rows = jnp.concatenate([query_pre_grad, key_pre_grad, own_values], axis=1).astype(
        jnp.bfloat16
    )
    joint_grad = jnp.einsum(
        "ld,lc->dc", attn_in, joint_grad_rows, preferred_element_type=jnp.float32
    )
    attn_in_grad = scatter_ordered(
        jnp.einsum(
            "lc,dc->ld", joint_grad_rows, joint_weight, preferred_element_type=jnp.float32
        ).astype(jnp.bfloat16)
    )
    tokens_part, attn_pre_grad = norm_back(residual, gains[0], attn_in_grad)
    tokens_grad = middle_grad + tokens_part
    small_grads = [
        jnp.pad(item.reshape(-1, gain_rows), ((0, 0), (0, rows - gain_rows))).reshape(-1)
        for item in (query_gain_grad, key_gain_grad)
    ]
    gain_grads = jnp.stack(
        [attn_pre_grad, attn_post_grad, ff_pre_grad, ff_post_grad] + small_grads, axis=1
    )
    gain_grads = jnp.pad(gain_grads, ((0, 0), (0, 128 - gain_grads.shape[1])))
    packed_grad = jnp.concatenate(
        [
            joint_grad[:, :head_size].astype(jnp.bfloat16),
            output_grad_turned.astype(jnp.bfloat16),
            joint_grad[:, head_size:].astype(jnp.bfloat16),
            gain_grads.astype(jnp.bfloat16),
        ],
        axis=1,
    )
    packed_grad, feed_forward_owned = lax.optimization_barrier((packed_grad, feed_forward_owned))
    down_owned = jnp.transpose(feed_forward_owned[0]).astype(jnp.float32)
    gate_up_owned = jnp.stack(feed_forward_owned[1:], axis=0).astype(jnp.float32)
    packed_owned = lax.psum_scatter(packed_grad, "dp", scatter_dimension=0, tiled=True)
    query_owned = packed_owned[:, :head_size].astype(jnp.float32)
    output_owned = jnp.transpose(packed_owned[:, head_size : 2 * head_size]).astype(jnp.float32)
    summed = sum_over_mp(packed_owned[:, 2 * head_size :])
    keyval_owned = summed[:, : 2 * head_size]
    gain_owned = jnp.transpose(summed[:, 2 * head_size :])
    return (
        result,
        tokens_grad,
        query_owned,
        keyval_owned,
        output_owned,
        gate_up_owned,
        down_owned,
        gain_owned[0],
        gain_owned[1],
        gain_owned[2],
        gain_owned[3],
        gain_owned[4, :gain_rows],
        gain_owned[5, :gain_rows],
    )


def solution(mesh):
    placed = (
        P(("dp", "mp"), None),
        P("dp"),
        P("dp"),
        P("dp", "mp"),
        P("dp", None),
        P("mp", "dp"),
        P(None, "dp", "mp"),
        P("mp", "dp"),
        P("dp"),
        P("dp"),
        P("dp"),
        P("dp"),
        P("dp"),
        P("dp"),
        P(("dp", "mp"), None),
    )
    return jax.shard_map(
        local,
        mesh=mesh,
        in_specs=placed,
        out_specs=(
            P(("dp", "mp"), None),
            P(("dp", "mp"), None),
            P("dp", "mp"),
            P("dp", None),
            P("mp", "dp"),
            P(None, "dp", "mp"),
            P("mp", "dp"),
            P("dp"),
            P("dp"),
            P("dp"),
            P("dp"),
            P("dp"),
            P("dp"),
        ),
        check_vma=False,
    )
```

profile of v0, /device:TPU:0, one launch (start us, length us, event | category | flops | bytes accessed | tf_op | source)
XLA Modules:
  0.0 732.3 jit_solution(13621012869615528322)
XLA Ops:
  14.2 56.9 %all-gather.4.cloned.1.call-done = bf16[1152,1152]{1,0:T(8,128)(2,1)} async-done(((bf16[144,1152]{1,0:T(8,128)(2,1)}), bf16[1152,1152]{1,0:T(8,128)(2,1)}) %all-gather.4.cloned.1.call-update) | async-done | bytes 2654224 | tf_op jit(solution)/shard_map/all_gather | solution.py:131
  80.4 9.1 %collective-permute-done.2 = bf16[128,1152]{1,0:T(8,128)(2,1)S(1)} collective-permute-done((bf16[128,1152]{1,0:T(8,128)(2,1)S(1)}, bf16[128,1152]{1,0:T(8,128)(2,1)S(1)}, u32[]{:S(2)}, u32[]{:S(2)}) %collective-permute-start.2) | collective-permute-done | bytes 294944 | tf_op jit(solution)/shard_map/ppermute | solution.py:20
  103.1 10.1 %collective-permute-start.5 = (bf16[512,256]{1,0:T(8,128)(2,1)S(1)}, bf16[512,256]{1,0:T(8,128)(2,1)S(1)}, u32[]{:S(2)}, u32[]{:S(2)}) collective-permute-start(bf16[512,256]{1,0:T(8,128)(2,1)S(1)} %slice.321), channel_id=1, source_target_pairs={{0,4},{4,8},{8,12},{12,16},{16,20},{20,24},{24,28},{1,5},{5,9},{9,... | collective-permute-start | bytes 786440 | tf_op jit(solution)/shard_map/ppermute | solution.py:15
  120.8 5.7 collective-permute-done.8
  126.5 7.6 %collective-permute-done.7 = bf16[128,1152]{1,0:T(8,128)(2,1)S(1)} collective-permute-done((bf16[128,1152]{1,0:T(8,128)(2,1)S(1)}, bf16[128,1152]{1,0:T(8,128)(2,1)S(1)}, u32[]{:S(2)}, u32[]{:S(2)}) %collective-permute-start.7) | collective-permute-done | bytes 294944 | tf_op jit(solution)/shard_map/ppermute | solution.py:20
  138.2 6.0 collective-permute-done.11
  149.7 54.7 %all-gather.6.cloned.1.call-done = bf16[2,1152,1728]{2,1,0:T(8,128)(2,1)} async-done(((bf16[2,144,1728]{2,1,0:T(8,128)(2,1)}), bf16[2,1152,1728]{2,1,0:T(8,128)(2,1)}) %all-gather.6.cloned.1.call-update) | async-done | bytes 7962640 | tf_op jit(solution)/shard_map/all_gather | solution.py:132
  211.4 6.8 multiply_convert_fusion.1
  218.2 59.2 %all-gather.8.cloned.1.call-done = bf16[1728,1152]{0,1:T(8,128)(2,1)} async-done(((bf16[1728,144]{0,1:T(8,128)(2,1)}), bf16[1728,1152]{0,1:T(8,128)(2,1)}) %all-gather.8.cloned.1.call-update) | async-done | bytes 3981328 | tf_op jit(solution)/shard_map/all_gather | solution.py:133
  277.4 5.3 convolution_convert_fusion.5
  289.2 9.2 %collective-permute-done.13 = bf16[128,1152]{1,0:T(8,128)(2,1)S(1)} collective-permute-done((bf16[128,1152]{1,0:T(8,128)(2,1)S(1)}, bf16[128,1152]{1,0:T(8,128)(2,1)S(1)}, u32[]{:S(2)}, u32[]{:S(2)}) %collective-permute-start.13) | collective-permute-done | bytes 294944 | tf_op jit(solution)/shard_map/ppermute | solution.py:20
  302.6 6.7 collective-permute-done.17
  318.6 8.4 %multiply_convert_fusion = (bf16[512,1728]{0,1:T(8,128)(2,1)S(1)}, bf16[512,1728]{0,1:T(8,128)(2,1)S(1)}) fusion(f32[512,1728]{0,1:T(8,128)S(1)} %copy-done.77, f32[512,1728]{0,1:T(8,128)} %get-tuple-element.185, bf16[1728,1152]{0,1:T(8,128)(2,1)S(1)} %copy-done.67, bf16[128,1152]{1,0:T(8,128)(2,1)S(1)} %collective-permute-done.17, ...), kind=kOutput, calls=%fused_computation.20 | convolution fusion | flops 2064384000 | bytes 15777792 | tf_op jit(solution)/shard_map/ld,fd->lf/dot_general | solution.py:213
  329.7 5.4 convolution_convert_fusion.1
  344.1 6.5 copy.60
  350.7 6.5 copy.62
  362.7 6.5 copy.64
  369.2 7.4 %collective-permute-done.19 = bf16[128,1152]{1,0:T(8,128)(2,1)} collective-permute-done((bf16[128,1152]{1,0:T(8,128)(2,1)}, bf16[128,1152]{1,0:T(8,128)(2,1)}, u32[]{:S(2)}, u32[]{:S(2)}) %collective-permute-start.19) | collective-permute-done | bytes 294944 | tf_op jit(solution)/shard_map/ppermute | solution.py:20
  388.4 6.6 collective-permute-done.22
  403.9 13.7 %collective-permute-done.24 = bf16[512,256]{1,0:T(8,128)(2,1)S(1)} collective-permute-done((bf16[512,256]{1,0:T(8,128)(2,1)S(1)}, bf16[512,256]{1,0:T(8,128)(2,1)S(1)}, u32[]{:S(2)}, u32[]{:S(2)}) %collective-permute-start.24) | collective-permute-done | bytes 262176 | tf_op jit(solution)/shard_map/ppermute | solution.py:15
  449.0 89.0 %reduce-scatter.15.cloned.1.call-done = bf16[144,1728]{1,0:T(8,128)(2,1)} async-done(((bf16[1152,1728]{1,0:T(8,128)(2,1)}), bf16[144,1728]{1,0:T(8,128)(2,1)}) %reduce-scatter.15.cloned.1.call-update) | async-done | bytes 497680
  540.2 88.7 %reduce-scatter.17.cloned.1.call-done = bf16[144,1728]{1,0:T(8,128)(2,1)} async-done(((bf16[1152,1728]{1,0:T(8,128)(2,1)}), bf16[144,1728]{1,0:T(8,128)(2,1)}) %reduce-scatter.17.cloned.1.call-update) | async-done | bytes 497680
  642.2 62.7 %reduce-scatter.19.cloned.1.call-done = bf16[144,1152]{1,0:T(8,128)(2,1)} async-done(((bf16[1152,1152]{1,0:T(8,128)(2,1)}), bf16[144,1152]{1,0:T(8,128)(2,1)}) %reduce-scatter.19.cloned.1.call-update) | async-done | bytes 331792
  713.1 9.9 %collective-permute-done.30 = bf16[144,640]{0,1:T(8,128)(2,1)S(1)} collective-permute-done((bf16[144,640]{0,1:T(8,128)(2,1)S(1)}, bf16[144,640]{0,1:T(8,128)(2,1)S(1)}, u32[]{:S(2)}, u32[]{:S(2)}) %collective-permute-start.30) | collective-permute-done | bytes 184352 | tf_op jit(solution)/shard_map/ppermute | solution.py:20
  (360 shorter events, 168.2 us)
Async XLA Ops:
  7.2 63.9 %all-gather.4.cloned.1.call-start = ((), (), s32[]{:S(2)}) async-start(), calls=%async_computation.4 | async-start | bytes 2985984 | tf_op jit(solution)/shard_map/all_gather | solution.py:131
  13.2 191.2 %all-gather.6.cloned.1.call-start = ((), (), s32[]{:S(2)}) async-start(), calls=%async_computation.5 | async-start | bytes 9289728 | tf_op jit(solution)/shard_map/all_gather | solution.py:132
  13.9 263.5 %all-gather.8.cloned.1.call-start = ((), (), s32[]{:S(2)}) async-start(), calls=%async_computation.6 | async-start | bytes 4644864 | tf_op jit(solution)/shard_map/all_gather | solution.py:133
  74.2 372.5 %reduce-scatter.13.cloned.1.call-start = ((), (), s32[]{:S(2)}) async-start(), calls=%async_computation.7 | async-start | bytes 4644864
  74.5 15.0 %collective-permute-start.2 = (bf16[128,1152]{1,0:T(8,128)(2,1)S(1)}, bf16[128,1152]{1,0:T(8,128)(2,1)S(1)}, u32[]{:S(2)}, u32[]{:S(2)}) collective-permute-start(bf16[128,1152]{1,0:T(8,128)(2,1)S(1)} %get-tuple-element.141), channel_id=1, source_target_pairs={{0,2},{1,3},{2,0},{3,1},{4,6},{5,7},{6,4},{7,5},{8,10},{9,11},{10,... | collective-permute-start | bytes 884744 | tf_op jit(solution)/shard_map/ppermute | solution.py:20
  76.0 13.8 %collective-permute-start.3 = (bf16[128,1152]{1,0:T(8,128)(2,1)S(1)}, bf16[128,1152]{1,0:T(8,128)(2,1)S(1)}, u32[]{:S(2)}, u32[]{:S(2)}) collective-permute-start(bf16[128,1152]{1,0:T(8,128)(2,1)S(1)} %get-tuple-element.141), channel_id=1, source_target_pairs={{0,1},{1,2},{2,3},{3,0},{4,5},{5,6},{6,7},{7,4},{8,9},{9,10},{10,1... | collective-permute-start | bytes 884744 | tf_op jit(solution)/shard_map/ppermute | solution.py:20
  94.9 18.2 %collective-permute-start.4 = (bf16[512,256]{1,0:T(8,128)(2,1)S(1)}, bf16[512,256]{1,0:T(8,128)(2,1)S(1)}, u32[]{:S(2)}, u32[]{:S(2)}) collective-permute-start(bf16[512,256]{1,0:T(8,128)(2,1)S(1)} %pad_maximum_fusion.9), channel_id=1, source_target_pairs={{0,4},{4,8},{8,12},{12,16},{16,20},{20,24},{24,28},{1,5},{5,9},{9,... | collective-permute-start | bytes 786440 | tf_op jit(solution)/shard_map/ppermute | solution.py:15
  103.1 13.9 %collective-permute-start.5 = (bf16[512,256]{1,0:T(8,128)(2,1)S(1)}, bf16[512,256]{1,0:T(8,128)(2,1)S(1)}, u32[]{:S(2)}, u32[]{:S(2)}) collective-permute-start(bf16[512,256]{1,0:T(8,128)(2,1)S(1)} %slice.321), channel_id=1, source_target_pairs={{0,4},{4,8},{8,12},{12,16},{16,20},{20,24},{24,28},{1,5},{5,9},{9,... | collective-permute-start | bytes 786440 | tf_op jit(solution)/shard_map/ppermute | solution.py:15
  119.6 14.6 %collective-permute-start.7 = (bf16[128,1152]{1,0:T(8,128)(2,1)S(1)}, bf16[128,1152]{1,0:T(8,128)(2,1)S(1)}, u32[]{:S(2)}, u32[]{:S(2)}) collective-permute-start(bf16[128,1152]{1,0:T(8,128)(2,1)S(1)} %get-tuple-element.159), channel_id=1, source_target_pairs={{0,2},{1,3},{2,0},{3,1},{4,6},{5,7},{6,4},{7,5},{8,10},{9,11},{10,... | collective-permute-start | bytes 884744 | tf_op jit(solution)/shard_map/ppermute | solution.py:20
  120.6 14.1 %collective-permute-start.6 = (bf16[128,1152]{1,0:T(8,128)(2,1)S(1)}, bf16[128,1152]{1,0:T(8,128)(2,1)S(1)}, u32[]{:S(2)}, u32[]{:S(2)}) collective-permute-start(bf16[128,1152]{1,0:T(8,128)(2,1)S(1)} %get-tuple-element.157), channel_id=1, source_target_pairs={{0,1},{1,2},{2,3},{3,0},{4,5},{5,6},{6,7},{7,4},{8,9},{9,10},{10,1... | collective-permute-start | bytes 884744 | tf_op jit(solution)/shard_map/ppermute | solution.py:20
  282.9 15.5 %collective-permute-start.13 = (bf16[128,1152]{1,0:T(8,128)(2,1)S(1)}, bf16[128,1152]{1,0:T(8,128)(2,1)S(1)}, u32[]{:S(2)}, u32[]{:S(2)}) collective-permute-start(bf16[128,1152]{1,0:T(8,128)(2,1)S(1)} %get-tuple-element.156), channel_id=1, source_target_pairs={{0,2},{1,3},{2,0},{3,1},{4,6},{5,7},{6,4},{7,5},{8,10},{9,11},{10,... | collective-permute-start | bytes 884744 | tf_op jit(solution)/shard_map/ppermute | solution.py:20
  284.4 14.1 %collective-permute-start.12 = (bf16[128,1152]{1,0:T(8,128)(2,1)S(1)}, bf16[128,1152]{1,0:T(8,128)(2,1)S(1)}, u32[]{:S(2)}, u32[]{:S(2)}) collective-permute-start(bf16[128,1152]{1,0:T(8,128)(2,1)S(1)} %get-tuple-element.154), channel_id=1, source_target_pairs={{0,1},{1,2},{2,3},{3,0},{4,5},{5,6},{6,7},{7,4},{8,9},{9,10},{10,1... | collective-permute-start | bytes 884744 | tf_op jit(solution)/shard_map/ppermute | solution.py:20
  350.6 187.4 %reduce-scatter.15.cloned.1.call-start = ((), (), s32[]{:S(2)}) async-start(), calls=%async_computation.8 | async-start | bytes 4644864
  357.2 271.7 %reduce-scatter.17.cloned.1.call-start = ((), (), s32[]{:S(2)}) async-start(), calls=%async_computation.9 | async-start | bytes 4644864
  361.2 15.4 %collective-permute-start.19 = (bf16[128,1152]{1,0:T(8,128)(2,1)}, bf16[128,1152]{1,0:T(8,128)(2,1)}, u32[]{:S(2)}, u32[]{:S(2)}) collective-permute-start(bf16[128,1152]{1,0:T(8,128)(2,1)} %get-tuple-element.153), channel_id=1, source_target_pairs={{0,2},{1,3},{2,0},{3,1},{4,6},{5,7},{6,4},{7,5},{8,10},{9,11},{10,... | collective-permute-start | bytes 884744 | tf_op jit(solution)/shard_map/ppermute | solution.py:20
  362.7 14.0 %collective-permute-start.18 = (bf16[128,1152]{1,0:T(8,128)(2,1)}, bf16[128,1152]{1,0:T(8,128)(2,1)}, u32[]{:S(2)}, u32[]{:S(2)}) collective-permute-start(bf16[128,1152]{1,0:T(8,128)(2,1)} %get-tuple-element.151), channel_id=1, source_target_pairs={{0,1},{1,2},{2,3},{3,0},{4,5},{5,6},{6,7},{7,4},{8,9},{9,10},{10,1... | collective-permute-start | bytes 884744 | tf_op jit(solution)/shard_map/ppermute | solution.py:20
  369.2 335.7 %reduce-scatter.19.cloned.1.call-start = ((), (), s32[]{:S(2)}) async-start(), calls=%async_computation.10 | async-start | bytes 2985984
  381.2 13.8 %collective-permute-start.22 = (bf16[128,1152]{1,0:T(8,128)(2,1)S(1)}, bf16[128,1152]{1,0:T(8,128)(2,1)S(1)}, u32[]{:S(2)}, u32[]{:S(2)}) collective-permute-start(bf16[128,1152]{1,0:T(8,128)(2,1)S(1)} %get-tuple-element.132), channel_id=1, source_target_pairs={{0,2},{1,3},{2,0},{3,1},{4,6},{5,7},{6,4},{7,5},{8,10},{9,11},{10,... | collective-permute-start | bytes 884744 | tf_op jit(solution)/shard_map/ppermute | solution.py:20
  381.9 14.1 %collective-permute-start.23 = (bf16[128,1152]{1,0:T(8,128)(2,1)S(1)}, bf16[128,1152]{1,0:T(8,128)(2,1)S(1)}, u32[]{:S(2)}, u32[]{:S(2)}) collective-permute-start(bf16[128,1152]{1,0:T(8,128)(2,1)S(1)} %get-tuple-element.132), channel_id=1, source_target_pairs={{0,1},{1,2},{2,3},{3,0},{4,5},{5,6},{6,7},{7,4},{8,9},{9,10},{10,1... | collective-permute-start | bytes 884744 | tf_op jit(solution)/shard_map/ppermute | solution.py:20
  397.2 22.6 %collective-permute-start.25 = (bf16[512,256]{1,0:T(8,128)(2,1)S(1)}, bf16[512,256]{1,0:T(8,128)(2,1)S(1)}, u32[]{:S(2)}, u32[]{:S(2)}) collective-permute-start(bf16[512,256]{1,0:T(8,128)(2,1)S(1)} %slice.319), channel_id=1, source_target_pairs={{4,0},{8,4},{12,8},{16,12},{20,16},{24,20},{28,24},{5,1},{9,5},{13... | collective-permute-start | bytes 786440 | tf_op jit(solution)/shard_map/ppermute | solution.py:15
  400.6 16.9 %collective-permute-start.24 = (bf16[512,256]{1,0:T(8,128)(2,1)S(1)}, bf16[512,256]{1,0:T(8,128)(2,1)S(1)}, u32[]{:S(2)}, u32[]{:S(2)}) collective-permute-start(bf16[512,256]{1,0:T(8,128)(2,1)S(1)} %slice.320), channel_id=1, source_target_pairs={{4,0},{8,4},{12,8},{16,12},{20,16},{24,20},{28,24},{5,1},{9,5},{13... | collective-permute-start | bytes 786440 | tf_op jit(solution)/shard_map/ppermute | solution.py:15
  422.3 14.2 %collective-permute-start.26 = (bf16[128,1152]{1,0:T(8,128)(2,1)S(1)}, bf16[128,1152]{1,0:T(8,128)(2,1)}, u32[]{:S(2)}, u32[]{:S(2)}) collective-permute-start(bf16[128,1152]{1,0:T(8,128)(2,1)S(1)} %get-tuple-element.148), channel_id=1, source_target_pairs={{0,1},{1,2},{2,3},{3,0},{4,5},{5,6},{6,7},{7,4},{8,9},{9,10},{10,1... | collective-permute-start | bytes 884744 | tf_op jit(solution)/shard_map/ppermute | solution.py:20
  706.1 16.9 %collective-permute-start.30 = (bf16[144,640]{0,1:T(8,128)(2,1)S(1)}, bf16[144,640]{0,1:T(8,128)(2,1)S(1)}, u32[]{:S(2)}, u32[]{:S(2)}) collective-permute-start(bf16[144,640]{0,1:T(8,128)(2,1)S(1)} %copy.69), channel_id=1, source_target_pairs={{0,2},{1,3},{2,0},{3,1},{4,6},{5,7},{6,4},{7,5},{8,10},{9,11},{10,... | collective-permute-start | bytes 552968 | tf_op jit(solution)/shard_map/ppermute | solution.py:20
  707.6 15.5 %collective-permute-start.29 = (bf16[144,640]{0,1:T(8,128)(2,1)S(1)}, bf16[144,640]{0,1:T(8,128)(2,1)S(1)}, u32[]{:S(2)}, u32[]{:S(2)}) collective-permute-start(bf16[144,640]{0,1:T(8,128)(2,1)S(1)} %copy.69), channel_id=1, source_target_pairs={{0,1},{1,2},{2,3},{3,0},{4,5},{5,6},{6,7},{7,4},{8,9},{9,10},{10,1... | collective-permute-start | bytes 552968 | tf_op jit(solution)/shard_map/ppermute | solution.py:20
  (97 other events, 906.3 us)
Sparse Core Ops, SparseCore 0:
  13.3 57.7 all-gather.3
  73.3 131.1 all-gather.5
  206.6 70.7 all-gather.7
  350.7 95.9 reduce-scatter.12
  450.5 87.4 reduce-scatter.14
  541.4 87.4 reduce-scatter.16
  634.6 70.2 reduce-scatter.18
where the time goes:
time: 740 us; the launch traced here: 732 us
  waiting for transfers between devices  533 us (72%)
  local copies, waits for them, and re-layouts  65.2 us (9%)
  matrix products  59.8 us (8%)
  starting transfers between devices  36.2 us (5%)
  other arithmetic  22.5 us (3%)
  between operations  15.8 us (2%)
    unnamed x11, waiting for transfers between devices  246 us
    ppermute x27, waiting for transfers between devices, shifted(): lax.ppermute(value, axis, [(i, (i + shift) % count) for i in range(count)])  99.2 us
    all_gather x1, waiting for transfers between devices, local(): down_full = lax.all_gather(down_weight, 'dp', axis=1, tiled=True)  59.2 us
    all_gather x1, waiting for transfers between devices, local(): packed_full = lax.all_gather(packed, 'dp', axis=0, tiled=True)  56.9 us
    all_gather x1, waiting for transfers between devices, local(): gate_up_full = lax.all_gather(gate_up_weight, 'dp', axis=1, tiled=True)  54.7 us
    unnamed x175, local copies, waits for them, and re-layouts  34.6 us
    ppermute x5, starting transfers between devices, from_behind(): lax.ppermute(value, axis, [(source, source + steps) for source in range(l...  19.4 us
    ppermute x5, waiting for transfers between devices, from_behind(): lax.ppermute(value, axis, [(source, source + steps) for source in range(l...  17.3 us
  transfers between devices with their start and end apart: 39, of which 34 were waited for; matrix products, arithmetic and copies ran while one was open for 11% of the time, Pallas kernels for 0%

commit v1 on v0

--- a/solution.py
+++ b/solution.py
@@ -128,7 +128,12 @@
     )
     gain_columns = jnp.pad(gain_columns, ((0, 0), (0, 128 - gain_columns.shape[1])))
     packed = jnp.concatenate([q_weight, kv_weight, jnp.transpose(o_weight), gain_columns], axis=1)
-    packed_full = lax.all_gather(packed, "dp", axis=0, tiled=True)
+    ring = [packed]
+    for hop in range(7):
+        ring.append(lax.ppermute(ring[-1], "dp", [(dev, (dev + 1) % 8) for dev in range(8)]))
+    packed_full = jnp.roll(
+        jnp.concatenate(ring[::-1], axis=0), (lax.axis_index("dp") + 1) * ring[0].shape[0], axis=0
+    )
     gate_up_full = lax.all_gather(gate_up_weight, "dp", axis=1, tiled=True)
     down_full = lax.all_gather(down_weight, "dp", axis=1, tiled=True)
     joint_weight = packed_full[:, : 3 * head_size]

time: 740 us -> 732 us (0.989)
  waiting for transfers between devices: 533 us -> 499 us
  matrix products: 59.8 us -> 71.2 us
  starting transfers between devices: 36.2 us -> 45.2 us
    ppermute x0 -> x7, waiting for transfers between devices: none -> 119 us  [local(): lax.ppermute(ring[-1], 'dp', [(dev, (dev + 1) % 8) for dev in range(8)])]
    all_gather x1 -> x0, waiting for transfers between devices: 56.9 us -> none  [local(): packed_full = lax.all_gather(packed, 'dp', axis=0, tiled=True)]
    all_gather x1, waiting for transfers between devices: 54.7 us -> 0.01 us  [local(): gate_up_full = lax.all_gather(gate_up_weight, 'dp', axis=1, tiled=True)]
    all_gather x1, waiting for transfers between devices: 59.2 us -> 12.9 us  [local(): down_full = lax.all_gather(down_weight, 'dp', axis=1, tiled=True)]
    dot_general x1, matrix products: 8.38 us -> 16.7 us  [local(): jnp.einsum('ld,fd->lf', ff_grad_all, down_full, preferred_element_type=jn...]
    unnamed x175 -> x195, local copies, waits for them, and re-layouts: 34.6 us -> 38.7 us
    unnamed x11 -> x10, waiting for transfers between devices: 246 us -> 247 us
  transfers between devices with their start and end apart: 39 -> 45, of which waited for: 34 -> 39; matrix products, arithmetic and copies ran while one was open for 11% -> 13% of each run, Pallas kernels for 0% -> 0%
where the time goes in v1:
time: 732 us; the launch traced here: 723 us
  waiting for transfers between devices  499 us (68%)
  matrix products  71.2 us (10%)
  local copies, waits for them, and re-layouts  69 us (9%)
  starting transfers between devices  45.2 us (6%)
  other arithmetic  22 us (3%)
  between operations  16.1 us (2%)
    unnamed x10, waiting for transfers between devices  247 us
    ppermute x7, waiting for transfers between devices, local(): lax.ppermute(ring[-1], 'dp', [(dev, (dev + 1) % 8) for dev in range(8)])  119 us
    ppermute x27, waiting for transfers between devices, shifted(): lax.ppermute(value, axis, [(i, (i + shift) % count) for i in range(count)])  99 us
    unnamed x195, local copies, waits for them, and re-layouts  38.7 us
    ppermute x5, starting transfers between devices, from_behind(): lax.ppermute(value, axis, [(source, source + steps) for source in range(l...  23.5 us
    ppermute x5, waiting for transfers between devices, from_behind(): lax.ppermute(value, axis, [(source, source + steps) for source in range(l...  22 us
    ppermute x27, starting transfers between devices, shifted(): lax.ppermute(value, axis, [(i, (i + shift) % count) for i in range(count)])  17.5 us
    dot_general x1, matrix products, local(): jnp.einsum('ld,fd->lf', ff_grad_all, down_full, preferred_element_type=jn...  16.7 us
  transfers between devices with their start and end apart: 45, of which 39 were waited for; matrix products, arithmetic and copies ran while one was open for 13% of the time, Pallas kernels for 0%

profile of v1, /device:TPU:0, one launch (start us, length us, event | category | flops | bytes accessed | tf_op | source)
XLA Modules:
  0.0 722.7 jit_solution(11633733469663234833)
XLA Ops:
  16.1 11.0 %collective-permute-done.1 = bf16[144,1152]{1,0:T(8,128)(2,1)S(1)} collective-permute-done((bf16[144,1152]{1,0:T(8,128)(2,1)S(1)}, bf16[144,1152]{1,0:T(8,128)(2,1)S(1)}, u32[]{:S(2)}, u32[]{:S(2)}) %collective-permute-start.1) | collective-permute-done | bytes 331808 | tf_op jit(solution)/shard_map/ppermute | solution.py:133
  28.1 18.9 %collective-permute-done.2 = bf16[144,1152]{1,0:T(8,128)(2,1)S(1)} collective-permute-done((bf16[144,1152]{1,0:T(8,128)(2,1)S(1)}, bf16[144,1152]{1,0:T(8,128)(2,1)S(1)}, u32[]{:S(2)}, u32[]{:S(2)}) %collective-permute-start.2) | collective-permute-done | bytes 331808 | tf_op jit(solution)/shard_map/ppermute | solution.py:133
  47.0 19.5 %collective-permute-done.3 = bf16[144,1152]{1,0:T(8,128)(2,1)S(1)} collective-permute-done((bf16[144,1152]{1,0:T(8,128)(2,1)S(1)}, bf16[144,1152]{1,0:T(8,128)(2,1)S(1)}, u32[]{:S(2)}, u32[]{:S(2)}) %collective-permute-start.3) | collective-permute-done | bytes 331808 | tf_op jit(solution)/shard_map/ppermute | solution.py:133
  66.5 15.3 %collective-permute-done.4 = bf16[144,1152]{1,0:T(8,128)(2,1)S(1)} collective-permute-done((bf16[144,1152]{1,0:T(8,128)(2,1)S(1)}, bf16[144,1152]{1,0:T(8,128)(2,1)S(1)}, u32[]{:S(2)}, u32[]{:S(2)}) %collective-permute-start.4) | collective-permute-done | bytes 331808 | tf_op jit(solution)/shard_map/ppermute | solution.py:133
  81.8 17.5 %collective-permute-done.5 = bf16[144,1152]{1,0:T(8,128)(2,1)S(1)} collective-permute-done((bf16[144,1152]{1,0:T(8,128)(2,1)S(1)}, bf16[144,1152]{1,0:T(8,128)(2,1)S(1)}, u32[]{:S(2)}, u32[]{:S(2)}) %collective-permute-start.5) | collective-permute-done | bytes 331808 | tf_op jit(solution)/shard_map/ppermute | solution.py:133
  99.3 18.6 %collective-permute-done.6 = bf16[144,1152]{1,0:T(8,128)(2,1)S(1)} collective-permute-done((bf16[144,1152]{1,0:T(8,128)(2,1)S(1)}, bf16[144,1152]{1,0:T(8,128)(2,1)S(1)}, u32[]{:S(2)}, u32[]{:S(2)}) %collective-permute-start.6) | collective-permute-done | bytes 331808 | tf_op jit(solution)/shard_map/ppermute | solution.py:133
  119.1 18.0 %collective-permute-done.7 = bf16[144,1152]{1,0:T(8,128)(2,1)S(1)} collective-permute-done((bf16[144,1152]{1,0:T(8,128)(2,1)S(1)}, bf16[144,1152]{1,0:T(8,128)(2,1)S(1)}, u32[]{:S(2)}, u32[]{:S(2)}) %collective-permute-start.7) | collective-permute-done | bytes 331808 | tf_op jit(solution)/shard_map/ppermute | solution.py:133
  148.7 9.1 %collective-permute-done.9 = bf16[128,1152]{1,0:T(8,128)(2,1)S(1)} collective-permute-done((bf16[128,1152]{1,0:T(8,128)(2,1)S(1)}, bf16[128,1152]{1,0:T(8,128)(2,1)S(1)}, u32[]{:S(2)}, u32[]{:S(2)}) %collective-permute-start.9) | collective-permute-done | bytes 294944 | tf_op jit(solution)/shard_map/ppermute | solution.py:20
  164.9 13.2 %collective-permute-start = (bf16[512]{0:T(512)(128)(2,1)S(1)}, bf16[512]{0:T(512)(128)(2,1)S(1)}, u32[]{:S(2)}, u32[]{:S(2)}) collective-permute-start(bf16[512]{0:T(512)(128)(2,1)S(1)} %add_convert_fusion.1), channel_id=1, source_target_pairs={{0,4},{4,8},{8,12},{12,16},{16,20},{20,24},{24,28},{1,5},{5,9},{9,... | collective-permute-start | bytes 3080 | tf_op jit(solution)/shard_map/ppermute | solution.py:15
  187.4 6.7 collective-permute-done.12
  203.1 9.3 %collective-permute-done.14 = bf16[128,1152]{1,0:T(8,128)(2,1)S(1)} collective-permute-done((bf16[128,1152]{1,0:T(8,128)(2,1)S(1)}, bf16[128,1152]{1,0:T(8,128)(2,1)S(1)}, u32[]{:S(2)}, u32[]{:S(2)}) %collective-permute-start.14) | collective-permute-done | bytes 294944 | tf_op jit(solution)/shard_map/ppermute | solution.py:20
  216.5 6.4 collective-permute-done.18
  235.1 6.7 multiply_convert_fusion.1
  241.8 12.9 %all-gather.5.cloned.1.call-done = bf16[1728,1152]{0,1:T(8,128)(2,1)} async-done(((bf16[1728,144]{0,1:T(8,128)(2,1)}), bf16[1728,1152]{0,1:T(8,128)(2,1)}) %all-gather.5.cloned.1.call-update) | async-done | bytes 3981328 | tf_op jit(solution)/shard_map/all_gather | solution.py:138
  266.6 9.1 %collective-permute-done.20 = bf16[128,1152]{1,0:T(8,128)(2,1)S(1)} collective-permute-done((bf16[128,1152]{1,0:T(8,128)(2,1)S(1)}, bf16[128,1152]{1,0:T(8,128)(2,1)S(1)}, u32[]{:S(2)}, u32[]{:S(2)}) %collective-permute-start.20) | collective-permute-done | bytes 294944 | tf_op jit(solution)/shard_map/ppermute | solution.py:20
  279.9 6.7 collective-permute-done.24
  296.0 16.7 %multiply_convert_fusion = (bf16[512,1728]{0,1:T(8,128)(2,1)S(1)}, bf16[512,1728]{0,1:T(8,128)(2,1)S(1)}) fusion(f32[512,1728]{0,1:T(8,128)S(1)} %copy-done.80, f32[512,1728]{0,1:T(8,128)} %get-tuple-element.185, bf16[1728,1152]{0,1:T(8,128)(2,1)S(1)} %copy-done.70, bf16[128,1152]{1,0:T(8,128)(2,1)S(1)} %collective-permute-done.24, ...), kind=kOutput, calls=%fused_computation.20 | convolution fusion | flops 2064384000 | bytes 15777792 | tf_op jit(solution)/shard_map/ld,fd->lf/dot_general | solution.py:218
  329.9 6.5 copy.60
  354.9 7.4 %collective-permute-done.26 = bf16[128,1152]{1,0:T(8,128)(2,1)} collective-permute-done((bf16[128,1152]{1,0:T(8,128)(2,1)}, bf16[128,1152]{1,0:T(8,128)(2,1)}, u32[]{:S(2)}, u32[]{:S(2)}) %collective-permute-start.26) | collective-permute-done | bytes 294944 | tf_op jit(solution)/shard_map/ppermute | solution.py:20
  390.7 13.9 %collective-permute-done.31 = bf16[512,256]{1,0:T(8,128)(2,1)S(1)} collective-permute-done((bf16[512,256]{1,0:T(8,128)(2,1)S(1)}, bf16[512,256]{1,0:T(8,128)(2,1)S(1)}, u32[]{:S(2)}, u32[]{:S(2)}) %collective-permute-start.31) | collective-permute-done | bytes 262176 | tf_op jit(solution)/shard_map/ppermute | solution.py:15
  438.9 88.8 %reduce-scatter.15.cloned.1.call-done = bf16[144,1728]{1,0:T(8,128)(2,1)} async-done(((bf16[1152,1728]{1,0:T(8,128)(2,1)}), bf16[144,1728]{1,0:T(8,128)(2,1)}) %reduce-scatter.15.cloned.1.call-update) | async-done | bytes 497680
  530.0 88.5 %reduce-scatter.17.cloned.1.call-done = bf16[144,1728]{1,0:T(8,128)(2,1)} async-done(((bf16[1152,1728]{1,0:T(8,128)(2,1)}), bf16[144,1728]{1,0:T(8,128)(2,1)}) %reduce-scatter.17.cloned.1.call-update) | async-done | bytes 497680
  631.8 63.2 %reduce-scatter.19.cloned.1.call-done = bf16[144,1152]{1,0:T(8,128)(2,1)} async-done(((bf16[1152,1152]{1,0:T(8,128)(2,1)}), bf16[144,1152]{1,0:T(8,128)(2,1)}) %reduce-scatter.19.cloned.1.call-update) | async-done | bytes 331792
  703.3 9.8 %collective-permute-done.37 = bf16[144,640]{0,1:T(8,128)(2,1)S(1)} collective-permute-done((bf16[144,640]{0,1:T(8,128)(2,1)S(1)}, bf16[144,640]{0,1:T(8,128)(2,1)S(1)}, u32[]{:S(2)}, u32[]{:S(2)}) %collective-permute-start.37) | collective-permute-done | bytes 184352 | tf_op jit(solution)/shard_map/ppermute | solution.py:20
  (393 shorter events, 212.6 us)
Async XLA Ops:
  7.2 220.8 %all-gather.3.cloned.1.call-start = ((), (), s32[]{:S(2)}) async-start(), calls=%async_computation.4 | async-start | bytes 9289728 | tf_op jit(solution)/shard_map/all_gather | solution.py:137
  7.9 246.8 %all-gather.5.cloned.1.call-start = ((), (), s32[]{:S(2)}) async-start(), calls=%async_computation.5 | async-start | bytes 4644864 | tf_op jit(solution)/shard_map/all_gather | solution.py:138
  27.2 19.8 %collective-permute-start.2 = (bf16[144,1152]{1,0:T(8,128)(2,1)S(1)}, bf16[144,1152]{1,0:T(8,128)(2,1)S(1)}, u32[]{:S(2)}, u32[]{:S(2)}) collective-permute-start(bf16[144,1152]{1,0:T(8,128)(2,1)S(1)} %collective-permute-done.1), channel_id=1, source_target_pairs={{0,4},{4,8},{8,12},{12,16},{16,20},{20,24},{24,28},{28,0},{1,5},{5... | collective-permute-start | bytes 995336 | tf_op jit(solution)/shard_map/ppermute | solution.py:133
  47.0 19.5 %collective-permute-start.3 = (bf16[144,1152]{1,0:T(8,128)(2,1)S(1)}, bf16[144,1152]{1,0:T(8,128)(2,1)S(1)}, u32[]{:S(2)}, u32[]{:S(2)}) collective-permute-start(bf16[144,1152]{1,0:T(8,128)(2,1)S(1)} %collective-permute-done.2), channel_id=1, source_target_pairs={{0,4},{4,8},{8,12},{12,16},{16,20},{20,24},{24,28},{28,0},{1,5},{5... | collective-permute-start | bytes 995336 | tf_op jit(solution)/shard_map/ppermute | solution.py:133
  66.5 15.3 %collective-permute-start.4 = (bf16[144,1152]{1,0:T(8,128)(2,1)S(1)}, bf16[144,1152]{1,0:T(8,128)(2,1)S(1)}, u32[]{:S(2)}, u32[]{:S(2)}) collective-permute-start(bf16[144,1152]{1,0:T(8,128)(2,1)S(1)} %collective-permute-done.3), channel_id=1, source_target_pairs={{0,4},{4,8},{8,12},{12,16},{16,20},{20,24},{24,28},{28,0},{1,5},{5... | collective-permute-start | bytes 995336 | tf_op jit(solution)/shard_map/ppermute | solution.py:133
  81.8 17.5 %collective-permute-start.5 = (bf16[144,1152]{1,0:T(8,128)(2,1)S(1)}, bf16[144,1152]{1,0:T(8,128)(2,1)S(1)}, u32[]{:S(2)}, u32[]{:S(2)}) collective-permute-start(bf16[144,1152]{1,0:T(8,128)(2,1)S(1)} %collective-permute-done.4), channel_id=1, source_target_pairs={{0,4},{4,8},{8,12},{12,16},{16,20},{20,24},{24,28},{28,0},{1,5},{5... | collective-permute-start | bytes 995336 | tf_op jit(solution)/shard_map/ppermute | solution.py:133
  99.3 18.6 %collective-permute-start.6 = (bf16[144,1152]{1,0:T(8,128)(2,1)S(1)}, bf16[144,1152]{1,0:T(8,128)(2,1)S(1)}, u32[]{:S(2)}, u32[]{:S(2)}) collective-permute-start(bf16[144,1152]{1,0:T(8,128)(2,1)S(1)} %collective-permute-done.5), channel_id=1, source_target_pairs={{0,4},{4,8},{8,12},{12,16},{16,20},{20,24},{24,28},{28,0},{1,5},{5... | collective-permute-start | bytes 995336 | tf_op jit(solution)/shard_map/ppermute | solution.py:133
  118.0 19.1 %collective-permute-start.7 = (bf16[144,1152]{1,0:T(8,128)(2,1)S(1)}, bf16[144,1152]{1,0:T(8,128)(2,1)S(1)}, u32[]{:S(2)}, u32[]{:S(2)}) collective-permute-start(bf16[144,1152]{1,0:T(8,128)(2,1)S(1)} %collective-permute-done.6), channel_id=1, source_target_pairs={{0,4},{4,8},{8,12},{12,16},{16,20},{20,24},{24,28},{28,0},{1,5},{5... | collective-permute-start | bytes 995336 | tf_op jit(solution)/shard_map/ppermute | solution.py:133
  142.5 294.1 %reduce-scatter.13.cloned.1.call-start = ((), (), s32[]{:S(2)}) async-start(), calls=%async_computation.6 | async-start | bytes 4644864
  142.6 15.2 %collective-permute-start.9 = (bf16[128,1152]{1,0:T(8,128)(2,1)S(1)}, bf16[128,1152]{1,0:T(8,128)(2,1)S(1)}, u32[]{:S(2)}, u32[]{:S(2)}) collective-permute-start(bf16[128,1152]{1,0:T(8,128)(2,1)S(1)} %get-tuple-element.141), channel_id=1, source_target_pairs={{0,2},{1,3},{2,0},{3,1},{4,6},{5,7},{6,4},{7,5},{8,10},{9,11},{10,... | collective-permute-start | bytes 884744 | tf_op jit(solution)/shard_map/ppermute | solution.py:20
  163.6 22.3 %collective-permute-start.11 = (bf16[512,256]{1,0:T(8,128)(2,1)S(1)}, bf16[512,256]{1,0:T(8,128)(2,1)S(1)}, u32[]{:S(2)}, u32[]{:S(2)}) collective-permute-start(bf16[512,256]{1,0:T(8,128)(2,1)S(1)} %pad_maximum_fusion.9), channel_id=1, source_target_pairs={{0,4},{4,8},{8,12},{12,16},{16,20},{20,24},{24,28},{1,5},{5,9},{9,... | collective-permute-start | bytes 786440 | tf_op jit(solution)/shard_map/ppermute | solution.py:15
  164.9 14.4 %collective-permute-start = (bf16[512]{0:T(512)(128)(2,1)S(1)}, bf16[512]{0:T(512)(128)(2,1)S(1)}, u32[]{:S(2)}, u32[]{:S(2)}) collective-permute-start(bf16[512]{0:T(512)(128)(2,1)S(1)} %add_convert_fusion.1), channel_id=1, source_target_pairs={{0,4},{4,8},{8,12},{12,16},{16,20},{20,24},{24,28},{1,5},{5,9},{9,... | collective-permute-start | bytes 3080 | tf_op jit(solution)/shard_map/ppermute | solution.py:15
  179.4 14.7 %collective-permute-start.12 = (bf16[512,256]{1,0:T(8,128)(2,1)S(1)}, bf16[512,256]{1,0:T(8,128)(2,1)S(1)}, u32[]{:S(2)}, u32[]{:S(2)}) collective-permute-start(bf16[512,256]{1,0:T(8,128)(2,1)S(1)} %slice.309), channel_id=1, source_target_pairs={{0,4},{4,8},{8,12},{12,16},{16,20},{20,24},{24,28},{1,5},{5,9},{9,... | collective-permute-start | bytes 786440 | tf_op jit(solution)/shard_map/ppermute | solution.py:15
  196.8 15.6 %collective-permute-start.14 = (bf16[128,1152]{1,0:T(8,128)(2,1)S(1)}, bf16[128,1152]{1,0:T(8,128)(2,1)S(1)}, u32[]{:S(2)}, u32[]{:S(2)}) collective-permute-start(bf16[128,1152]{1,0:T(8,128)(2,1)S(1)} %get-tuple-element.159), channel_id=1, source_target_pairs={{0,2},{1,3},{2,0},{3,1},{4,6},{5,7},{6,4},{7,5},{8,10},{9,11},{10,... | collective-permute-start | bytes 884744 | tf_op jit(solution)/shard_map/ppermute | solution.py:20
  260.2 15.5 %collective-permute-start.20 = (bf16[128,1152]{1,0:T(8,128)(2,1)S(1)}, bf16[128,1152]{1,0:T(8,128)(2,1)S(1)}, u32[]{:S(2)}, u32[]{:S(2)}) collective-permute-start(bf16[128,1152]{1,0:T(8,128)(2,1)S(1)} %get-tuple-element.156), channel_id=1, source_target_pairs={{0,2},{1,3},{2,0},{3,1},{4,6},{5,7},{6,4},{7,5},{8,10},{9,11},{10,... | collective-permute-start | bytes 884744 | tf_op jit(solution)/shard_map/ppermute | solution.py:20
  336.3 191.4 %reduce-scatter.15.cloned.1.call-start = ((), (), s32[]{:S(2)}) async-start(), calls=%async_computation.7 | async-start | bytes 4644864
  342.9 275.7 %reduce-scatter.17.cloned.1.call-start = ((), (), s32[]{:S(2)}) async-start(), calls=%async_computation.8 | async-start | bytes 4644864
  346.9 15.4 %collective-permute-start.26 = (bf16[128,1152]{1,0:T(8,128)(2,1)}, bf16[128,1152]{1,0:T(8,128)(2,1)}, u32[]{:S(2)}, u32[]{:S(2)}) collective-permute-start(bf16[128,1152]{1,0:T(8,128)(2,1)} %get-tuple-element.153), channel_id=1, source_target_pairs={{0,2},{1,3},{2,0},{3,1},{4,6},{5,7},{6,4},{7,5},{8,10},{9,11},{10,... | collective-permute-start | bytes 884744 | tf_op jit(solution)/shard_map/ppermute | solution.py:20
  354.8 340.2 %reduce-scatter.19.cloned.1.call-start = ((), (), s32[]{:S(2)}) async-start(), calls=%async_computation.9 | async-start | bytes 2985984
  384.0 22.9 %collective-permute-start.32 = (bf16[512,256]{1,0:T(8,128)(2,1)S(1)}, bf16[512,256]{1,0:T(8,128)(2,1)S(1)}, u32[]{:S(2)}, u32[]{:S(2)}) collective-permute-start(bf16[512,256]{1,0:T(8,128)(2,1)S(1)} %slice.307), channel_id=1, source_target_pairs={{4,0},{8,4},{12,8},{16,12},{20,16},{24,20},{28,24},{5,1},{9,5},{13... | collective-permute-start | bytes 786440 | tf_op jit(solution)/shard_map/ppermute | solution.py:15
  387.5 17.1 %collective-permute-start.31 = (bf16[512,256]{1,0:T(8,128)(2,1)S(1)}, bf16[512,256]{1,0:T(8,128)(2,1)S(1)}, u32[]{:S(2)}, u32[]{:S(2)}) collective-permute-start(bf16[512,256]{1,0:T(8,128)(2,1)S(1)} %slice.308), channel_id=1, source_target_pairs={{4,0},{8,4},{12,8},{16,12},{20,16},{24,20},{28,24},{5,1},{9,5},{13... | collective-permute-start | bytes 786440 | tf_op jit(solution)/shard_map/ppermute | solution.py:15
  410.3 15.1 %collective-permute-start.34 = (bf16[128,1152]{1,0:T(8,128)(2,1)S(1)}, bf16[128,1152]{1,0:T(8,128)(2,1)S(1)}, u32[]{:S(2)}, u32[]{:S(2)}) collective-permute-start(bf16[128,1152]{1,0:T(8,128)(2,1)S(1)} %get-tuple-element.150), channel_id=1, source_target_pairs={{0,2},{1,3},{2,0},{3,1},{4,6},{5,7},{6,4},{7,5},{8,10},{9,11},{10,... | collective-permute-start | bytes 884744 | tf_op jit(solution)/shard_map/ppermute | solution.py:20
  696.2 16.9 %collective-permute-start.37 = (bf16[144,640]{0,1:T(8,128)(2,1)S(1)}, bf16[144,640]{0,1:T(8,128)(2,1)S(1)}, u32[]{:S(2)}, u32[]{:S(2)}) collective-permute-start(bf16[144,640]{0,1:T(8,128)(2,1)S(1)} %copy.69), channel_id=1, source_target_pairs={{0,2},{1,3},{2,0},{3,1},{4,6},{5,7},{6,4},{7,5},{8,10},{9,11},{10,... | collective-permute-start | bytes 552968 | tf_op jit(solution)/shard_map/ppermute | solution.py:20
  697.7 15.5 %collective-permute-start.36 = (bf16[144,640]{0,1:T(8,128)(2,1)S(1)}, bf16[144,640]{0,1:T(8,128)(2,1)S(1)}, u32[]{:S(2)}, u32[]{:S(2)}) collective-permute-start(bf16[144,640]{0,1:T(8,128)(2,1)S(1)} %copy.69), channel_id=1, source_target_pairs={{0,1},{1,2},{2,3},{3,0},{4,5},{5,6},{6,7},{7,4},{8,9},{9,10},{10,1... | collective-permute-start | bytes 552968 | tf_op jit(solution)/shard_map/ppermute | solution.py:20
  (106 other events, 1007.1 us)
Sparse Core Ops, SparseCore 0:
  10.2 164.5 all-gather.2
  177.0 77.6 all-gather.4
  336.5 100.1 reduce-scatter.12
  440.5 87.2 reduce-scatter.14
  531.2 87.2 reduce-scatter.16
  624.2 70.7 reduce-scatter.18
